TPU v7x, 512 devices: a whole 4x8x8 slice. The times are simulated.
512 devices in a mesh: dp: 64 (over y, z_lo, core), tensor: 8 (over z_hi, x).
Axes of the slice: x: 4, y: 8, z: 8 (z_hi: 2, z_lo: 4; z = z_hi * 4 + z_lo), core: 2. Of those that a mesh axis runs over, the one named last changes fastest.
Arguments:
- acts: bfloat16 [65536, 7168], P('dp', 'tensor'), may hold values from -6 to 6
- targets: bfloat16 [65536, 384], P('dp'), may hold values from -6 to 6
- probe: int32 [7168, 384], P('tensor'), may hold values from 0 to 1
- master: float32 [7168, 384], P(('tensor', 'dp')), may hold values from -0.28347334 to 0.28347334
- moment: float32 [7168, 384], P(('tensor', 'dp')), may hold values from -0.6 to 0.6
- curv: float32 [7168, 384], P(('tensor', 'dp')), may hold values from 0.05 to 2
Outputs:
- new_weight: bfloat16 [7168, 384], P('tensor')
- moment_out: float32 [7168, 384], P(('tensor', 'dp'))
- curv_out: float32 [7168, 384], P(('tensor', 'dp'))
All inputs are finite; a program needn't handle non-finite values.
Results may differ from a plain program's by a relative error of at most 0.0053.
Values may be sent and summed in bfloat16 or wider, within the bound.
A program may use at most 64 MiB of HBM per device.

v0:
```python
import math

import jax
import jax.numpy as jnp
from jax import lax
from jax.sharding import PartitionSpec as P


def body(acts, targets, probe, master, moment, curv):
    shard_rows = master.shape[0]
    columns = master.shape[1]
    tokens_all = acts.shape[0] * lax.axis_size("dp")
    inverse = 1.0 / math.sqrt(tokens_all)
    weight_low = master.astype(jnp.bfloat16)
    out_part = jnp.dot(
        acts,
        lax.all_gather(weight_low, "dp", axis=0, tiled=True),
        preferred_element_type=jnp.float32,
    )
    signs = (2 * probe - 1).astype(jnp.bfloat16)
    probe_part = jnp.dot(acts, signs, preferred_element_type=jnp.float32)
    out_full, probe_full = lax.psum((out_part, probe_part), "tensor")
    slope = jnp.tanh(out_full - targets.astype(jnp.float32))
    bend = (1.0 - slope * slope) * probe_full
    signals = jnp.concatenate([slope * inverse, bend * inverse], axis=1).astype(jnp.bfloat16)

    def contract(signal_part):
        return lax.dot_general(
            acts, signal_part, (((0,), (0,)), ((), ())), preferred_element_type=jnp.float32
        )

    grad = lax.psum_scatter(contract(signals[:, :columns]), "dp", scatter_dimension=0, tiled=True)
    hvp = lax.psum_scatter(contract(signals[:, columns:]), "dp", scatter_dimension=0, tiled=True)
    probe_rows = lax.dynamic_slice_in_dim(probe, lax.axis_index("dp") * shard_rows, shard_rows, 0)
    estimate = (2 * probe_rows - 1).astype(jnp.float32) * hvp
    moment_out = 0.9 * moment + 0.1 * grad
    curv_out = 0.9 * curv + 0.1 * estimate
    step = jnp.clip(moment_out / jnp.maximum(0.05 * curv_out, 0.02), -1.0, 1.0)
    updated = (master - 0.02 * (step + 0.1 * master)).astype(jnp.bfloat16)
    new_weight = lax.all_gather(updated, "dp", axis=0, tiled=True)
    return (new_weight, moment_out, curv_out)


def solution(mesh):
    in_specs = (
        P("dp", "tensor"),
        P("dp", None),
        P("tensor", None),
        P(("tensor", "dp"), None),
        P(("tensor", "dp"), None),
        P(("tensor", "dp"), None),
    )
    out_specs = (P("tensor", None), P(("tensor", "dp"), None), P(("tensor", "dp"), None))
    return jax.shard_map(body, mesh=mesh, in_specs=in_specs, out_specs=out_specs, check_vma=False)
```

profile of v0, /device:TPU:1, one launch (start us, length us, event | category | flops | bytes accessed | tf_op | source)
XLA Modules:
  0.0 902.3 jit_solution(17430847060961604071)
XLA Ops:
  7.2 0.0 copy-start
  7.2 0.0 all-reduce.9.cloned.1.call-start
  7.2 0.9 convert_bitcast_fusion
  8.1 85.9 %all-gather = bf16[64,14,384]{2,1,0:T(8,128)(2,1)S(1)} all-gather(bf16[1,14,384]{2,1,0:T(8,128)(2,1)S(1)} %convert_bitcast_fusion), channel_id=1, replica_groups=mesh['dp'=64,'tensor'=8] {'dp'}, dimensions={0}, use_global_device_ids=true | all-gather | bytes 698880 | tf_op jit(solution)/shard_map/all_gather | solution.py:17
  94.0 0.2 reshape.7
  94.2 0.0 copy-start.7
  94.2 2.3 fusion.11
  96.6 2.4 convolution_bitcast_fusion
  98.9 0.0 all-reduce.9.cloned.1.call-update
  99.0 0.0 all-reduce.7.cloned.1.call-start
  99.0 172.7 %all-reduce.9.cloned.1.call-done = (f32[1024,384]{1,0:T(8,128)}, f32[1024,384]{1,0:T(8,128)}) async-done(((f32[1024,384]{1,0:T(8,128)}, f32[1024,384]{1,0:T(8,128)}), (f32[1024,384]{1,0:T(8,128)}, f32[1024,384]{1,0:T(8,128)})) %all-reduce.9.cloned.1.call-update) | async-done | bytes 3145744 | tf_op jit(solution)/shard_map/psum | solution.py:22
  271.7 0.0 copy-done.2
  271.7 3.7 convolution_bitcast_fusion.2
  275.4 2.2 convolution_bitcast_fusion.1
  277.7 0.0 all-reduce.7.cloned.1.call-update
  277.7 1.3 dynamic-slice
  279.6 532.9 %all-reduce.7.cloned.1.call-done = (f32[896,384]{0,1:T(8,128)}, f32[896,384]{0,1:T(8,128)}) async-done(((f32[896,384]{0,1:T(8,128)}, f32[896,384]{0,1:T(8,128)}), (f32[896,384]{0,1:T(8,128)}, f32[896,384]{0,1:T(8,128)})) %all-reduce.7.cloned.1.call-update) | async-done | bytes 2752528
  812.6 1.3 constant_dynamic-slice_fusion
  813.8 0.1 copy.42
  813.9 0.1 copy.44
  814.1 0.0 copy-done.6
  814.1 1.4 fusion.5
  815.5 78.9 %all-gather.1 = bf16[64,14,384]{2,1,0:T(8,128)(2,1)S(1)} all-gather(bf16[1,14,384]{2,1,0:T(8,128)(2,1)S(1)} %get-tuple-element.16), channel_id=1, replica_groups=mesh['dp'=64,'tensor'=8] {'dp'}, dimensions={0}, use_global_device_ids=true | all-gather | bytes 698880 | tf_op jit(solution)/shard_map/all_gather | solution.py:40
  894.4 1.0 reshape.9
  (12 shorter events, 0.0 us)
Async XLA Ops:
  7.2 87.1 %copy-start = (bf16[1024,896]{1,0:T(8,128)(2,1)S(1)}, bf16[1024,896]{1,0:T(8,128)(2,1)}, u32[]{:S(2)}) copy-start(bf16[1024,896]{1,0:T(8,128)(2,1)} %param.6) | copy-start | bytes 5505028
  7.2 264.5 %all-reduce.9.cloned.1.call-start = ((), (), s32[]{:S(2)}) async-start(), calls=%async_computation.1 | async-start | bytes 6291456 | tf_op jit(solution)/shard_map/psum | solution.py:22
  94.2 2.3 copy-start.7
  98.9 172.8 %copy-start.2 = (bf16[1024,384]{1,0:T(8,128)(2,1)S(1)}, bf16[1024,384]{1,0:T(8,128)(2,1)}, u32[]{:S(2)}) copy-start(bf16[1024,384]{1,0:T(8,128)(2,1)} %param.7) | copy-start | bytes 2359300
  99.0 713.6 %all-reduce.7.cloned.1.call-start = ((), (), s32[]{:S(2)}) async-start(), calls=%async_computation | async-start | bytes 5505024
  271.7 3.7 copy-start.1
  271.7 3.7 copy-start.3
  277.6 536.4 %copy-start.4 = (f32[14,384]{1,0:T(8,128)S(1)}, f32[14,384]{1,0:T(8,128)}, u32[]{:S(2)}) copy-start(f32[14,384]{1,0:T(8,128)} %param.9) | copy-start | bytes 64516
  277.6 536.4 %copy-start.5 = (f32[14,384]{1,0:T(8,128)S(1)}, f32[14,384]{1,0:T(8,128)}, u32[]{:S(2)}) copy-start(f32[14,384]{1,0:T(8,128)} %param.11) | copy-start | bytes 64516
  277.6 536.4 %copy-start.6 = (f32[14,384]{1,0:T(8,128)S(1)}, f32[14,384]{1,0:T(8,128)}, u32[]{:S(2)}) copy-start(f32[14,384]{1,0:T(8,128)} %param.10) | copy-start | bytes 64516
Sparse Core Ops, SparseCore 0:
  99.1 172.5 all-reduce.8
  277.8 534.7 all-reduce.6
where the time goes:
time: 903 us; the launch traced here: 902 us
  waiting for transfers between devices  706 us (78%)
  blocking collectives  165 us (18%)
  between operations  14.8 us (2%)
  matrix products  10.6 us (1%)
    unnamed x3, waiting for transfers between devices  533 us
    psum x1, waiting for transfers between devices, body(): out_full, probe_full = lax.psum((out_part, probe_part), 'tensor')  173 us
    all_gather x1, blocking collectives, body(): lax.all_gather(weight_low, 'dp', axis=0, tiled=True)  85.9 us
    all_gather x1, blocking collectives, body(): new_weight = lax.all_gather(updated, 'dp', axis=0, tiled=True)  78.9 us
  transfers between devices with their start and end apart: 2, of which 2 were waited for; matrix products, arithmetic and copies ran while one was open for 0% of the time, Pallas kernels for 0%

commit v1 on v0

v1 whole, which is shorter than its diff:
```python
import math

import jax
import jax.numpy as jnp
from jax import lax
from jax.experimental import pallas as pl
from jax.experimental.pallas import tpu as pltpu
from jax.sharding import PartitionSpec as P

MESH = pl.DeviceIdType.MESH
F32 = jnp.float32
BF16 = jnp.bfloat16
NJ = 3
W = 128
A_, B_, C_, D_, E_, F_, Z_ = range(7)


def mm(a, b):
    return lax.dot_general(a, b, (((1,), (0,)), ((), ())), preferred_element_type=F32)


def mm_t(a, b):
    return lax.dot_general(a, b, (((1,), (1,)), ((), ())), preferred_element_type=F32)


def kernel(
    acts_hbm, targets_hbm, probe_hbm, master_ref, moment_ref, curv_ref,
    new_hbm, moment_out, curv_out,
    acts, probe, targets, signs, acts_pad, acts_t, sel, sel_t,
    master16, moment16, curv16, signs16,
    wbuf, nbuf, sig, obuf,
    s0, r0, s1, r1, keep0, own0, keep1, own1, tot0, tot1, probed,
    dsend, drecv, town, ysend, yrecv, ysum, zsend, zrecv,
    local_sem, rs_ss, rs_rs, ag_ss, ag_rs,
    wz_ss, wz_rs, wy_ss, wy_rs, wc_ss, wc_rs,
    d_ss, d_rs, y_ss, y_rs, z_ss, z_rs,
):
    inverse = 1.0 / math.sqrt(acts_hbm.shape[0] * lax.axis_size("dp"))
    dp = lax.axis_index("dp")
    tensor = lax.axis_index("tensor")
    y, zl, c = dp // 8, (dp // 2) % 4, dp % 2
    zh, x = tensor // 4, tensor % 4
    right, left, opp = (x + 1) % 4, (x + 3) % 4, (x + 2) % 4

    def dev(y_=None, zl_=None, c_=None, zh_=None, x_=None):
        y_ = y if y_ is None else y_
        zl_ = zl if zl_ is None else zl_
        c_ = c if c_ is None else c_
        zh_ = zh if zh_ is None else zh_
        x_ = x if x_ is None else x_
        return (y_ * 8 + zl_ * 2 + c_, zh_ * 4 + x_)

    to_right, to_left = dev(x_=right), dev(x_=left)
    to_zh, to_core = dev(zh_=1 - zh), dev(c_=1 - c)
    to_zl = [dev(zl_=(zl + i) % 4) for i in range(1, 4)]
    to_y = [dev(y_=(y + i) % 8) for i in range(1, 8)]
    own16 = pl.multiple_of(c * 512 + y * 64 + zl * 16, 16)
    own64 = pl.multiple_of(c * 512 + y * 64, 64)
    own512 = pl.multiple_of(c * 512, 512)

    def rcopy(src, dst, ss, rs, to):
        return pltpu.make_async_remote_copy(
            src_ref=src, dst_ref=dst, send_sem=ss, recv_sem=rs, device_id=to, device_id_type=MESH
        )

    sent = []

    def send(src, dst, ss, rs, to):
        copy = rcopy(src, dst, ss, rs, to)
        copy.start()
        sent.append(copy)

    def arrived(dst, rs):
        rcopy(dst, dst, rs, rs, to_core).wait_recv()

    def rows256(q):
        return pl.ds(pl.multiple_of(q * 256, 256), 256)

    loads = []
    probe_load = pltpu.make_async_copy(probe_hbm, probe, local_sem.at[0])
    probe_load.start()
    act_loads = []
    for n, q in enumerate((opp, right, left, x)):
        load = pltpu.make_async_copy(
            acts_hbm.at[rows256(q), :], acts.at[rows256(q), :], local_sem.at[1 + n]
        )
        load.start()
        act_loads.append(load)
    my_rows = pl.ds(pl.multiple_of(x * 256 + zh * 128, 128), 128)
    target_load = pltpu.make_async_copy(targets_hbm.at[my_rows, :], targets, local_sem.at[5])
    target_load.start()

    barrier = pltpu.get_barrier_semaphore()
    partners = [to_right, to_left, to_zh, to_core] + to_zl + to_y
    for to in partners:
        pl.semaphore_signal(barrier, inc=1, device_id=to, device_id_type=MESH)

    for padded, ref in ((master16, master_ref), (moment16, moment_ref), (curv16, curv_ref)):
        padded[...] = jnp.zeros_like(padded)
        padded[0:14, :] = ref[...]
    low = master16[...].astype(BF16)
    for j in range(NJ):
        wbuf[j, pl.ds(own16, 16), :] = low[:, j * W : (j + 1) * W]
    pl.semaphore_wait(barrier, len(partners))

    def gather_z(buf, k, j):
        rows = pl.ds(own16, 16)
        for i in range(3):
            send(buf.at[j, rows], buf.at[j, rows], wz_ss.at[k, j, i], wz_rs.at[k, j, i], to_zl[i])

    def gather_y(buf, k, j):
        for i in range(3):
            arrived(buf.at[j, pl.ds(0, 16)], wz_rs.at[k, j, i])
        rows = pl.ds(own64, 64)
        for i in range(7):
            send(buf.at[j, rows], buf.at[j, rows], wy_ss.at[k, j, i], wy_rs.at[k, j, i], to_y[i])

    def gather_core(buf, k, j):
        for i in range(7):
            arrived(buf.at[j, pl.ds(0, 64)], wy_rs.at[k, j, i])
        rows = pl.ds(own512, 512)
        send(buf.at[j, rows], buf.at[j, rows], wc_ss.at[k, j], wc_rs.at[k, j], to_core)

    def gathered(buf, k, j):
        arrived(buf.at[j, pl.ds(0, 512)], wc_rs.at[k, j])

    def bufs(g):
        if g == 0:
            return s0, r0, keep0, own0, tot0
        return s1.at[g - 1], r1.at[g - 1], keep1.at[g - 1], own1.at[g - 1], tot1.at[g - 1]

    def partial_sum(g, q, load):
        if g == 0:
            load.wait()
            return mm(acts[rows256(q), :], signs[...])
        return mm(acts_pad[rows256(q), :], wbuf[g - 1])

    def reduce_send(g, kind, to):
        sb, rb = bufs(g)[:2]
        send(sb.at[kind], rb.at[kind], rs_ss.at[g, kind], rs_rs.at[g, kind], to)

    def reduce_got(g, kind):
        rb = bufs(g)[1]
        arrived(rb.at[kind], rs_rs.at[g, kind])

    def reduce_1(g):
        sb, rb, keep, own, tot = bufs(g)
        part = partial_sum(g, opp, act_loads[0])
        sb[A_] = part[:128].astype(BF16)
        sb[B_] = part[128:].astype(BF16)
        reduce_send(g, A_, to_right)
        reduce_send(g, B_, to_left)
        part = partial_sum(g, right, act_loads[1])
        sb[C_] = part[128:].astype(BF16)
        reduce_send(g, C_, to_right)
        keep[0] = part[:128]
        part = partial_sum(g, left, act_loads[2])
        sb[D_] = part[:128].astype(BF16)
        reduce_send(g, D_, to_left)
        keep[1] = part[128:]
        own[...] = partial_sum(g, x, act_loads[3])

    def reduce_2(g):
        sb, rb, keep, own, tot = bufs(g)
        reduce_got(g, A_)
        sb[E_] = (keep[0] + rb[A_].astype(F32)).astype(BF16)
        reduce_send(g, E_, to_right)
        reduce_got(g, B_)
        sb[F_] = (keep[1] + rb[B_].astype(F32)).astype(BF16)
        reduce_send(g, F_, to_left)

    def reduce_3(g):
        sb, rb, keep, own, tot = bufs(g)
        for kind in (C_, D_, E_, F_):
            reduce_got(g, kind)
        tot[0] = own[0:128, :] + rb[E_].astype(F32) + rb[D_].astype(F32)
        tot[1] = own[128:256, :] + rb[C_].astype(F32) + rb[F_].astype(F32)
        sb[Z_] = tot[1 - zh].astype(BF16)
        reduce_send(g, Z_, to_zh)

    def reduce_4(g):
        sb, rb, keep, own, tot = bufs(g)
        reduce_got(g, Z_)
        return tot[zh] + rb[Z_].astype(F32)

    def piece(q, h):
        return pl.ds(pl.multiple_of(q * 256 + h * 128, 128), 128)

    def signal_send(j, q, h, idx, to):
        rows = piece(q, h)
        send(sig.at[j, rows], sig.at[j, rows], ag_ss.at[j, idx], ag_rs.at[j, idx], to)

    def signal_got(j, idx):
        arrived(sig.at[j, pl.ds(0, 128)], ag_rs.at[j, idx])

    def signal_a(j):
        out = reduce_4(1 + j)
        cols = slice(j * W, (j + 1) * W)
        slope = jnp.tanh(out - targets[:, cols].astype(F32))
        bend = (1.0 - slope * slope) * probed[:, cols]
        rows = piece(x, zh)
        sig[j, rows, 0:W] = (slope * inverse).astype(BF16)
        sig[j, rows, W : 2 * W] = (bend * inverse).astype(BF16)
        signal_send(j, x, zh, 0, to_zh)
        signal_send(j, x, zh, 1 + zh, to_right)
        signal_send(j, x, zh, 3 + zh, to_left)

    def signal_b(j):
        signal_got(j, 0)
        signal_send(j, x, 1 - zh, 2 - zh, to_right)
        signal_send(j, x, 1 - zh, 4 - zh, to_left)

    def signal_c(j):
        signal_got(j, 1)
        signal_send(j, left, 0, 5, to_right)
        signal_got(j, 4)
        signal_send(j, right, 1, 6, to_left)

    def signal_d(j):
        for idx in (2, 3, 5, 6):
            signal_got(j, idx)

    def terms_core(j):
        other = pl.ds(pl.multiple_of((1 - c) * 512, 512), 512)
        mine = pl.ds(own512, 512)
        dsend[j] = mm(acts_t[other, :], sig[j]).astype(BF16)
        send(dsend.at[j], drecv.at[j], d_ss.at[j], d_rs.at[j], to_core)
        town[j] = mm(acts_t[mine, :], sig[j])

    def terms_y(j):
        arrived(drecv.at[j], d_rs.at[j])
        town[j] = town[j] + drecv[j].astype(F32)
        ysend[j] = town[j].astype(BF16)
        for i in range(7):
            rows = pl.ds(pl.multiple_of(((y + 1 + i) % 8) * 64, 64), 64)
            send(ysend.at[j, rows], yrecv.at[j, i], y_ss.at[j, i], y_rs.at[j, i], to_y[i])

    def terms_z(j):
        for i in range(7):
            arrived(yrecv.at[j, i], y_rs.at[j, i])
        total = town[j, pl.ds(pl.multiple_of(y * 64, 64), 64), :]
        for i in range(7):
            total = total + yrecv[j, i].astype(F32)
        ysum[j] = total
        zsend[j] = total.astype(BF16)
        for i in range(3):
            rows = pl.ds(pl.multiple_of(((zl + 1 + i) % 4) * 16, 16), 16)
            send(zsend.at[j, rows], zrecv.at[j, i], z_ss.at[j, i], z_rs.at[j, i], to_zl[i])

    def update(j):
        for i in range(3):
            arrived(zrecv.at[j, i], z_rs.at[j, i])
        total = ysum[j, pl.ds(pl.multiple_of(zl * 16, 16), 16), :]
        for i in range(3):
            total = total + zrecv[j, i].astype(F32)
        grad, hvp = total[:, :W], total[:, W:]
        cols = slice(j * W, (j + 1) * W)
        estimate = signs16[:, cols] * hvp
        moment = 0.9 * moment16[:, cols] + 0.1 * grad
        curv = 0.9 * curv16[:, cols] + 0.1 * estimate
        moment_out[:, cols] = moment[0:14]
        curv_out[:, cols] = curv[0:14]
        step = jnp.clip(moment / jnp.maximum(0.05 * curv, 0.02), -1.0, 1.0)
        master = master16[:, cols]
        updated = master - 0.02 * (step + 0.1 * master)
        real = lax.broadcasted_iota(jnp.int32, updated.shape, 0) < 14
        nbuf[j, pl.ds(own16, 16), :] = jnp.where(real, updated, 0.0).astype(BF16)
        gather_z(nbuf, 1, j)

    stores = []

    def finish(j):
        gathered(nbuf, 1, j)
        obuf[j] = mm(sel_t[...], nbuf[j]).astype(BF16)
        store = pltpu.make_async_copy(
            obuf.at[j], new_hbm.at[:, pl.ds(j * W, W)], local_sem.at[6 + j]
        )
        store.start()
        stores.append(store)

    for j in range(NJ):
        gather_z(wbuf, 0, j)
    probe_load.wait()
    signs[...] = (2 * probe[...] - 1).astype(F32).astype(BF16)
    reduce_1(0)
    for j in range(NJ):
        gather_y(wbuf, 0, j)
    reduce_2(0)

    def source(p):
        r = p % 16
        row = (((p // 64) % 8) * 8 + ((p // 16) % 4) * 2 + p // 512) * 14 + r
        return jnp.where(r < 14, row, -1)

    @pl.loop(0, 7)
    def _(t):
        rows = pl.ds(pl.multiple_of(t * 128, 128), 128)
        k = lax.broadcasted_iota(jnp.int32, (128, 1024), 0) + t * 128
        p = source(lax.broadcasted_iota(jnp.int32, (1, 1024), 1))
        sel_t[rows, :] = jnp.where(k == p, 1.0, 0.0).astype(BF16)

    @pl.loop(0, 4)
    def _(t):
        rows = pl.ds(pl.multiple_of(t * 256, 256), 256)
        acts_pad[rows, :] = mm(acts[rows, :], sel_t[...]).astype(BF16)

    reduce_3(0)
    gather_core(wbuf, 0, 0)
    gathered(wbuf, 0, 0)
    reduce_1(1)
    gather_core(wbuf, 0, 1)
    reduce_2(1)
    gathered(wbuf, 0, 1)
    reduce_1(2)
    gather_core(wbuf, 0, 2)
    probed[...] = reduce_4(0)
    reduce_3(1)
    reduce_2(2)
    gathered(wbuf, 0, 2)
    reduce_1(3)

    @pl.loop(0, 8)
    def _(t):
        rows = pl.ds(pl.multiple_of(t * 128, 128), 128)
        k = lax.broadcasted_iota(jnp.int32, (128, 896), 1)
        p = source(lax.broadcasted_iota(jnp.int32, (128, 1), 0) + t * 128)
        sel[rows, :] = jnp.where(k == p, 1.0, 0.0).astype(BF16)

    target_load.wait()
    reduce_3(2)
    signal_a(0)
    reduce_2(3)

    @pl.loop(0, 4)
    def _(t):
        rows = pl.ds(pl.multiple_of(t * 256, 256), 256)
        acts_t[rows, :] = mm_t(sel[rows, :], acts[...]).astype(BF16)

    signs16[...] = mm(sel[pl.ds(own16, 16), :], signs[...])
    reduce_3(3)
    signal_b(0)
    signal_a(1)
    signal_c(0)
    signal_a(2)
    signal_b(1)
    signal_d(0)
    terms_core(0)
    signal_c(1)
    signal_b(2)
    terms_y(0)
    signal_d(1)
    terms_core(1)
    signal_c(2)
    terms_z(0)
    terms_y(1)
    update(0)
    signal_d(2)
    terms_core(2)
    terms_z(1)
    gather_y(nbuf, 1, 0)
    terms_y(2)
    update(1)
    gather_core(nbuf, 1, 0)
    terms_z(2)
    gather_y(nbuf, 1, 1)
    finish(0)
    update(2)
    gather_core(nbuf, 1, 1)
    gather_y(nbuf, 1, 2)
    finish(1)
    gather_core(nbuf, 1, 2)
    finish(2)
    for store in stores:
        store.wait()
    for copy in sent:
        copy.wait_send()


def body(acts, targets, probe, master, moment, curv):
    any_spec = pl.BlockSpec(memory_space=pl.ANY)
    vmem_spec = pl.BlockSpec(memory_space=pltpu.VMEM)
    dma = pltpu.SemaphoreType.DMA
    vm = pltpu.VMEM
    return pl.pallas_call(
        kernel,
        out_shape=(
            jax.ShapeDtypeStruct((896, 384), BF16),
            jax.ShapeDtypeStruct((14, 384), F32),
            jax.ShapeDtypeStruct((14, 384), F32),
        ),
        in_specs=[any_spec, any_spec, any_spec, vmem_spec, vmem_spec, vmem_spec],
        out_specs=(any_spec, vmem_spec, vmem_spec),
        scratch_shapes=[
            vm((1024, 896), BF16), vm((896, 384), jnp.int32), vm((128, 384), BF16),
            vm((896, 384), BF16), vm((1024, 1024), BF16), vm((1024, 1024), BF16),
            vm((1024, 896), BF16), vm((896, 1024), BF16),
            vm((16, 384), F32), vm((16, 384), F32), vm((16, 384), F32), vm((16, 384), F32),
            vm((NJ, 1024, W), BF16), vm((NJ, 1024, W), BF16),
            vm((NJ, 1024, 2 * W), BF16), vm((NJ, 896, W), BF16),
            vm((7, 128, 384), BF16), vm((7, 128, 384), BF16),
            vm((NJ, 7, 128, W), BF16), vm((NJ, 7, 128, W), BF16),
            vm((2, 128, 384), F32), vm((256, 384), F32),
            vm((NJ, 2, 128, W), F32), vm((NJ, 256, W), F32),
            vm((2, 128, 384), F32), vm((NJ, 2, 128, W), F32), vm((128, 384), F32),
            vm((NJ, 512, 2 * W), BF16), vm((NJ, 512, 2 * W), BF16), vm((NJ, 512, 2 * W), F32),
            vm((NJ, 512, 2 * W), BF16), vm((NJ, 7, 64, 2 * W), BF16), vm((NJ, 64, 2 * W), F32),
            vm((NJ, 64, 2 * W), BF16), vm((NJ, 3, 16, 2 * W), BF16),
            dma((9,)), dma((4, 7)), dma((4, 7)), dma((NJ, 7)), dma((NJ, 7)),
            dma((2, NJ, 3)), dma((2, NJ, 3)), dma((2, NJ, 7)), dma((2, NJ, 7)),
            dma((2, NJ)), dma((2, NJ)),
            dma((NJ,)), dma((NJ,)), dma((NJ, 7)), dma((NJ, 7)), dma((NJ, 3)), dma((NJ, 3)),
        ],
        compiler_params=pltpu.CompilerParams(
            collective_id=0, has_side_effects=True, vmem_limit_bytes=56 * 2**20
        ),
        name="sophia",
    )(acts, targets, probe, master, moment, curv)


def solution(mesh):
    in_specs = (
        P("dp", "tensor"),
        P("dp", None),
        P("tensor", None),
        P(("tensor", "dp"), None),
        P(("tensor", "dp"), None),
        P(("tensor", "dp"), None),
    )
    out_specs = (P("tensor", None), P(("tensor", "dp"), None), P(("tensor", "dp"), None))
    return jax.shard_map(body, mesh=mesh, in_specs=in_specs, out_specs=out_specs, check_vma=False)
```

time: 903 us -> 110 us (0.12)
  waiting for transfers between devices: 706 us -> 0 us
  blocking collectives: 165 us -> 0 us
  Pallas kernels: 0 us -> 105 us
  between operations: 14.8 us -> 0.64 us
  matrix products: 10.6 us -> 0 us
    unnamed x3 -> x0, waiting for transfers between devices: 533 us -> none
    psum x1 -> x0, waiting for transfers between devices: 173 us -> none  [body(): out_full, probe_full = lax.psum((out_part, probe_part), 'tensor')]
    all_gather x2 -> x0, blocking collectives: 165 us -> none  [the longest x1 85.9 us: body(): lax.all_gather(weight_low, 'dp', axis=0, tiled=True)]
    pallas_call x0 -> x1, Pallas kernels: none -> 105 us  [body(): pl.pallas_call(kernel, out_shape=(jax.ShapeDtypeStruct((896, 384), BF16),...]
    dot_general x4 -> x0, matrix products: 10.6 us -> none  [the longest x2 5.92 us: contract(): lax.dot_general(acts, signal_part, (((0,), (0,)), ((), ())), preferred_el...]
  transfers between devices with their start and end apart: 2 -> 0, of which waited for: 2 -> 0; matrix products, arithmetic and copies ran while one was open for 0% -> 0% of each run, Pallas kernels for 0% -> 0%
where the time goes in v1:
time: 110 us
  Pallas kernels  105 us (95%)
  local copies, waits for them, and re-layouts  4.71 us (4%)
    pallas_call x1, Pallas kernels, body(): pl.pallas_call(kernel, out_shape=(jax.ShapeDtypeStruct((896, 384), BF16),...  105 us
    unnamed x3, local copies, waits for them, and re-layouts  4.71 us

profile of v1, /device:TPU:1, one launch (start us, length us, event | category | flops | bytes accessed | tf_op | source)
XLA Modules:
  0.0 110.0 jit_solution(6903786138362386697)
XLA Ops:
  0.6 104.6 %sophia.1 = (bf16[896,384]{1,0:T(8,128)(2,1)}, f32[14,384]{1,0:T(8,128)}, f32[14,384]{1,0:T(8,128)}) custom-call(bf16[1024,896]{1,0:T(8,128)(2,1)} %acts_hbm.1, bf16[1024,384]{1,0:T(8,128)(2,1)} %targets_hbm.1, s32[896,384]{1,0:T(8,128)} %probe_hbm.1, f32[14,384]{1,0:T(8,128)} %master_ref.1, f32[14,384]{1,0:T(8,128)} %moment_ref.1, f32[14,384]{1,0:T(8,128)} %curv_ref.1), custom_call_target="tpu_custom_call" | custom-call | tf_op jit(solution)/shard_map/sophia/pallas_call | solution.py:384
  105.3 2.0 %copy.12 = bf16[896,384]{1,0:T(8,128)(2,1)} copy(bf16[896,384]{1,0:T(8,128)(2,1)} %get-tuple-element.6) | data formatting | bytes 1376256
  107.3 1.3 %copy.13 = f32[14,384]{1,0:T(8,128)} copy(f32[14,384]{1,0:T(8,128)} %get-tuple-element.7) | data formatting | bytes 43008
  108.6 1.3 %copy.14 = f32[14,384]{1,0:T(8,128)} copy(f32[14,384]{1,0:T(8,128)} %get-tuple-element.8) | data formatting | bytes 43008

commit v2 on v1

v2 whole, which is shorter than its diff:
```python
import math

import jax
import jax.numpy as jnp
from jax import lax
from jax.experimental import pallas as pl
from jax.experimental.pallas import tpu as pltpu
from jax.sharding import PartitionSpec as P

MESH = pl.DeviceIdType.MESH
F32 = jnp.float32
BF16 = jnp.bfloat16
NJ = 3
W = 128
A_, B_, C_, D_, E_, F_, Z_ = range(7)


def mm(a, b):
    return lax.dot_general(a, b, (((1,), (0,)), ((), ())), preferred_element_type=F32)


def mm_t(a, b):
    return lax.dot_general(a, b, (((1,), (1,)), ((), ())), preferred_element_type=F32)


def kernel(
    acts_hbm, targets_hbm, probe_hbm, master_ref, moment_ref, curv_ref,
    new_hbm, moment_out, curv_out,
    acts, probe, targets, signs, acts_pad, sel_t,
    master16, moment16, curv16, signs16,
    wbuf, nbuf, sig, obuf,
    s0, r0, s1, r1, keep0, own0, keep1, own1, tot0, tot1, probed,
    dsend, drecv, town, tsend, recv_a1, recv_b1, sum_a, sum_b, send_a2, send_b2, recv_a2, recv_b2,
    local_sem, rs_ss, rs_rs, ag_ss, ag_rs,
    wa_ss, wa_rs, wc_ss, wc_rs, d_ss, d_rs, t_ss, t_rs,
):
    inverse = 1.0 / math.sqrt(acts_hbm.shape[0] * lax.axis_size("dp"))
    dp = lax.axis_index("dp")
    tensor = lax.axis_index("tensor")
    y, zl, c = dp // 8, (dp // 2) % 4, dp % 2
    zh, x = tensor // 4, tensor % 4
    right, left, opp = (x + 1) % 4, (x + 3) % 4, (x + 2) % 4

    def dev(y_=None, zl_=None, c_=None, zh_=None, x_=None):
        y_ = y if y_ is None else y_
        zl_ = zl if zl_ is None else zl_
        c_ = c if c_ is None else c_
        zh_ = zh if zh_ is None else zh_
        x_ = x if x_ is None else x_
        return (y_ * 8 + zl_ * 2 + c_, zh_ * 4 + x_)

    to_right, to_left = dev(x_=right), dev(x_=left)
    to_zh, to_core = dev(zh_=1 - zh), dev(c_=1 - c)
    to_zl = [dev(zl_=(zl + i) % 4) for i in range(1, 4)]
    to_y = [dev(y_=(y + i) % 8) for i in range(1, 8)]

    def ring(i):
        return (y + 4 + i // 4) % 8, (zl + 2 + i % 4) % 4

    def each_peer(send_to):
        def visit(i, _):
            i = i + jnp.where(i >= 18, 1, 0)
            send_to(i, *ring(i))
            return 0

        lax.fori_loop(0, 31, visit, 0)

    own16 = pl.multiple_of(c * 512 + y * 64 + zl * 16, 16)
    own512 = pl.multiple_of(c * 512, 512)

    def rcopy(src, dst, ss, rs, to):
        return pltpu.make_async_remote_copy(
            src_ref=src, dst_ref=dst, send_sem=ss, recv_sem=rs, device_id=to, device_id_type=MESH
        )

    sent, bulk = [], []

    def send(src, dst, sems, to):
        ss, rs, at = sems
        copy = rcopy(src, dst, ss.at[at], rs.at[at], to)
        copy.start()
        sent.append(copy)

    def arrived(dst, rs, at):
        rcopy(dst, dst, rs.at[at], rs.at[at], to_core).wait_recv()

    def rows256(q):
        return pl.ds(pl.multiple_of(q * 256, 256), 256)

    loads = []
    probe_load = pltpu.make_async_copy(probe_hbm, probe, local_sem.at[0])
    probe_load.start()
    act_loads = []
    for n, q in enumerate((opp, right, left, x)):
        load = pltpu.make_async_copy(
            acts_hbm.at[rows256(q), :], acts.at[rows256(q), :], local_sem.at[1 + n]
        )
        load.start()
        act_loads.append(load)
    my_rows = pl.ds(pl.multiple_of(x * 256 + zh * 128, 128), 128)
    target_load = pltpu.make_async_copy(targets_hbm.at[my_rows, :], targets, local_sem.at[5])
    target_load.start()

    barrier = pltpu.get_barrier_semaphore()
    near = [to_right, to_left, to_zh, to_core]
    for to in near:
        pl.semaphore_signal(barrier, inc=1, device_id=to, device_id_type=MESH)

    def greet(i, y_, zl_):
        pl.semaphore_signal(barrier, inc=1, device_id=dev(y_=y_, zl_=zl_), device_id_type=MESH)

    each_peer(greet)

    def meet():
        pl.semaphore_wait(barrier, len(near) + 31)

    def load_rows():
        for padded, ref in ((master16, master_ref), (moment16, moment_ref), (curv16, curv_ref)):
            padded[...] = jnp.zeros_like(padded)
            padded[0:14, :] = ref[...]
        low = master16[...].astype(BF16)
        for j in range(NJ):
            wbuf[j, pl.ds(own16, 16), :] = low[:, j * W : (j + 1) * W]

    def gather_all(buf, k, j, count=1):
        rows = pl.ds(own16, 16)
        js = pl.ds(j, count)

        def visit(i, y_, zl_):
            rcopy(
                buf.at[js, rows], buf.at[js, rows], wa_ss.at[k, j], wa_rs.at[k, j],
                dev(y_=y_, zl_=zl_),
            ).start()

        each_peer(visit)
        bulk.append((buf.at[js, pl.ds(0, 496)], wa_ss, (k, j)))

    def gather_core(buf, k, j, count=1):
        js = pl.ds(j, count)
        arrived(buf.at[js, pl.ds(0, 496)], wa_rs, (k, j))
        rows = pl.ds(own512, 512)
        send(buf.at[js, rows], buf.at[js, rows], (wc_ss, wc_rs, (k, j)), to_core)

    def gathered(buf, k, j, count=1):
        arrived(buf.at[pl.ds(j, count), pl.ds(0, 512)], wc_rs, (k, j))

    def bufs(g):
        if g == 0:
            return s0, r0, keep0, own0, tot0
        return s1.at[g - 1], r1.at[g - 1], keep1.at[g - 1], own1.at[g - 1], tot1.at[g - 1]

    def partial_sum(g, q, load):
        if g == 0:
            load.wait()
            return mm(acts[rows256(q), :], signs[...])
        return mm(acts_pad[rows256(q), :], wbuf[g - 1])

    def reduce_send(g, kind, to):
        sb, rb = bufs(g)[:2]
        send(sb.at[kind], rb.at[kind], (rs_ss, rs_rs, (g, kind,)), to)

    def reduce_got(g, kind):
        rb = bufs(g)[1]
        arrived(rb.at[kind], rs_rs, (g, kind,))

    def reduce_0(g):
        sb = bufs(g)[0]
        part = partial_sum(g, opp, act_loads[0])
        sb[A_] = part[:128].astype(BF16)
        sb[B_] = part[128:].astype(BF16)

    def reduce_1(g):
        sb, rb, keep, own, tot = bufs(g)
        reduce_send(g, A_, to_right)
        reduce_send(g, B_, to_left)
        part = partial_sum(g, right, act_loads[1])
        sb[C_] = part[128:].astype(BF16)
        reduce_send(g, C_, to_right)
        keep[0] = part[:128]
        part = partial_sum(g, left, act_loads[2])
        sb[D_] = part[:128].astype(BF16)
        reduce_send(g, D_, to_left)
        keep[1] = part[128:]
        own[...] = partial_sum(g, x, act_loads[3])

    def reduce_2(g):
        sb, rb, keep, own, tot = bufs(g)
        reduce_got(g, A_)
        sb[E_] = (keep[0] + rb[A_].astype(F32)).astype(BF16)
        reduce_send(g, E_, to_right)
        reduce_got(g, B_)
        sb[F_] = (keep[1] + rb[B_].astype(F32)).astype(BF16)
        reduce_send(g, F_, to_left)

    def reduce_3(g):
        sb, rb, keep, own, tot = bufs(g)
        for kind in (C_, D_, E_, F_):
            reduce_got(g, kind)
        tot[0] = own[0:128, :] + rb[E_].astype(F32) + rb[D_].astype(F32)
        tot[1] = own[128:256, :] + rb[C_].astype(F32) + rb[F_].astype(F32)
        sb[Z_] = tot[1 - zh].astype(BF16)
        reduce_send(g, Z_, to_zh)

    def reduce_4(g):
        sb, rb, keep, own, tot = bufs(g)
        reduce_got(g, Z_)
        return tot[zh] + rb[Z_].astype(F32)

    def piece(q, h):
        return pl.ds(pl.multiple_of(q * 256 + h * 128, 128), 128)

    def signal_send(j, q, h, idx, to):
        rows = piece(q, h)
        send(sig.at[j, rows], sig.at[j, rows], (ag_ss, ag_rs, (j, idx,)), to)

    def signal_got(j, idx):
        arrived(sig.at[j, pl.ds(0, 128)], ag_rs, (j, idx,))

    def signal_a(j):
        out = reduce_4(1 + j)
        cols = slice(j * W, (j + 1) * W)
        slope = jnp.tanh(out - targets[:, cols].astype(F32))
        bend = (1.0 - slope * slope) * probed[:, cols]
        rows = piece(x, zh)
        sig[j, rows, 0:W] = (slope * inverse).astype(BF16)
        sig[j, rows, W : 2 * W] = (bend * inverse).astype(BF16)
        signal_send(j, x, zh, 0, to_zh)
        signal_send(j, x, zh, 1 + zh, to_right)
        signal_send(j, x, zh, 3 + zh, to_left)

    def signal_b(j):
        signal_got(j, 0)
        signal_send(j, x, 1 - zh, 2 - zh, to_right)
        signal_send(j, x, 1 - zh, 4 - zh, to_left)

    def signal_c(j):
        signal_got(j, 1)
        signal_send(j, left, 0, 5, to_right)
        signal_got(j, 4)
        signal_send(j, right, 1, 6, to_left)

    def signal_d(j):
        for idx in (2, 3, 5, 6):
            signal_got(j, idx)

    def contract(rows, j):
        return lax.dot_general(
            acts_pad[:, rows], sig[j], (((0,), (0,)), ((), ())), preferred_element_type=F32
        )

    def terms_core(j):
        dsend[j] = contract(pl.ds(pl.multiple_of((1 - c) * 512, 512), 512), j).astype(BF16)
        send(dsend.at[j], drecv.at[j], (d_ss, d_rs, (j,)), to_core)
        town[j] = contract(pl.ds(own512, 512), j).reshape(8, 4, 16, 2 * W)

    def bulk_send(j, phase, pairs, whole):
        for src, dst, to in pairs:
            rcopy(src, dst, t_ss.at[j, phase], t_rs.at[j, phase], to).start()
        bulk.append((whole, t_ss, (j, phase)))

    def terms_1(j):
        arrived(drecv.at[j], d_rs, (j,))
        total = town[j] + drecv[j].astype(F32).reshape(8, 4, 16, 2 * W)
        town[j] = total
        tsend[j, 0] = total[..., :W].astype(BF16)
        tsend[j, 1] = total[..., W:].astype(BF16)
        bulk_send(
            j, 1,
            [(tsend.at[j, 1, :, (zl + 1 + i) % 4], recv_b1.at[j, i], to_zl[i]) for i in range(3)],
            recv_b1.at[j],
        )
        bulk_send(
            j, 0,
            [(tsend.at[j, 0, (y + 1 + i) % 8], recv_a1.at[j, i], to_y[i]) for i in range(7)],
            recv_a1.at[j],
        )

    def terms_2(j):
        arrived(recv_a1.at[j], t_rs, (j, 0))
        total = town[j, y, :, :, 0:W]
        for i in range(7):
            total = total + recv_a1[j, i].astype(F32)
        sum_a[j] = total
        send_a2[j] = total.astype(BF16)
        bulk_send(
            j, 2,
            [(send_a2.at[j, (zl + 1 + i) % 4], recv_a2.at[j, i], to_zl[i]) for i in range(3)],
            recv_a2.at[j],
        )
        arrived(recv_b1.at[j], t_rs, (j, 1))
        total = town[j, :, zl, :, W : 2 * W]
        for i in range(3):
            total = total + recv_b1[j, i].astype(F32)
        sum_b[j] = total
        send_b2[j] = total.astype(BF16)
        bulk_send(
            j, 3,
            [(send_b2.at[j, (y + 1 + i) % 8], recv_b2.at[j, i], to_y[i]) for i in range(7)],
            recv_b2.at[j],
        )

    def update(j):
        arrived(recv_a2.at[j], t_rs, (j, 2))
        grad = sum_a[j, zl]
        for i in range(3):
            grad = grad + recv_a2[j, i].astype(F32)
        arrived(recv_b2.at[j], t_rs, (j, 3))
        hvp = sum_b[j, y]
        for i in range(7):
            hvp = hvp + recv_b2[j, i].astype(F32)
        cols = slice(j * W, (j + 1) * W)
        estimate = signs16[:, cols] * hvp
        moment = 0.9 * moment16[:, cols] + 0.1 * grad
        curv = 0.9 * curv16[:, cols] + 0.1 * estimate
        moment_out[:, cols] = moment[0:14]
        curv_out[:, cols] = curv[0:14]
        step = jnp.clip(moment / jnp.maximum(0.05 * curv, 0.02), -1.0, 1.0)
        master = master16[:, cols]
        updated = master - 0.02 * (step + 0.1 * master)
        real = lax.broadcasted_iota(jnp.int32, updated.shape, 0) < 14
        nbuf[j, pl.ds(own16, 16), :] = jnp.where(real, updated, 0.0).astype(BF16)
        gather_all(nbuf, 1, j)

    stores = []

    def finish(j):
        gathered(nbuf, 1, j)
        obuf[j] = mm(sel_t[...], nbuf[j]).astype(BF16)
        store = pltpu.make_async_copy(
            obuf.at[j], new_hbm.at[:, pl.ds(j * W, W)], local_sem.at[6 + j]
        )
        store.start()
        stores.append(store)

    def source(p):
        r = p % 16
        row = (((p // 64) % 8) * 8 + ((p // 16) % 4) * 2 + p // 512) * 14 + r
        return jnp.where(r < 14, row, -1)

    def make_signs():
        probe_load.wait()
        signs[...] = (2 * probe[...] - 1).astype(F32).astype(BF16)

    def make_sel_t():
        @pl.loop(0, 7)
        def _(t):
            rows = pl.ds(pl.multiple_of(t * 128, 128), 128)
            k = lax.broadcasted_iota(jnp.int32, (128, 1024), 0) + t * 128
            p = source(lax.broadcasted_iota(jnp.int32, (1, 1024), 1))
            sel_t[rows, :] = jnp.where(k == p, 1.0, 0.0).astype(BF16)

    def make_acts_pad(first, last):
        @pl.loop(first, last)
        def _(t):
            rows = pl.ds(pl.multiple_of(t * 256, 256), 256)
            acts_pad[rows, :] = mm(acts[rows, :], sel_t[...]).astype(BF16)

    def make_signs16():
        p = source(lax.broadcasted_iota(jnp.int32, (16, 1), 0) + own16)
        k = lax.broadcasted_iota(jnp.int32, (16, 896), 1)
        signs16[...] = mm(jnp.where(k == p, 1.0, 0.0).astype(BF16), signs[...])

    def keep_probed():
        probed[...] = reduce_4(0)

    steps = [
        (load_rows,), (make_signs,), (reduce_0, 0), (meet,),
        (gather_all, wbuf, 0, 0), (reduce_1, 0), (gather_all, wbuf, 0, 1),
        (gather_all, wbuf, 0, 2),
        (make_sel_t,), (make_acts_pad, 0, 2), (reduce_2, 0), (make_acts_pad, 2, 4),
        (make_signs16,), (gather_core, wbuf, 0, 0), (reduce_3, 0), (gathered, wbuf, 0, 0),
        (reduce_0, 1), (reduce_1, 1), (gather_core, wbuf, 0, 1), (reduce_2, 1),
        (gathered, wbuf, 0, 1), (reduce_0, 2), (reduce_1, 2), (gather_core, wbuf, 0, 2),
        (keep_probed,), (reduce_3, 1), (gathered, wbuf, 0, 2), (reduce_0, 3), (reduce_1, 3),
        (reduce_2, 2), (target_load.wait,), (reduce_2, 3), (reduce_3, 2), (signal_a, 0),
        (reduce_3, 3), (signal_b, 0), (signal_a, 1), (signal_c, 0), (signal_a, 2),
        (signal_b, 1), (signal_b, 2), (signal_c, 1), (signal_d, 0), (terms_core, 0),
        (signal_c, 2), (terms_1, 0), (signal_d, 1), (terms_core, 1), (terms_1, 1),
        (signal_d, 2), (terms_core, 2), (terms_2, 0), (terms_1, 2), (terms_2, 1), (update, 0),
        (terms_2, 2), (update, 1), (update, 2), (gather_core, nbuf, 1, 0),
        (gather_core, nbuf, 1, 1), (finish, 0), (finish, 1), (gather_core, nbuf, 1, 2),
        (finish, 2),
    ]
    for step, *values in steps:
        step(*values)
    for store in stores:
        store.wait()
    for copy in sent:
        copy.wait_send()
    for ref, ss, at in bulk:
        rcopy(ref, ref, ss.at[at], ss.at[at], to_core).wait_send()


def copy_kernel(*refs):
    count = len(refs) // 2
    for n in range(count):
        refs[count + n][...] = refs[n][...]


def body(acts, targets, probe, master, moment, curv):
    any_spec = pl.BlockSpec(memory_space=pl.ANY)
    vmem_spec = pl.BlockSpec(memory_space=pltpu.VMEM)
    dma = pltpu.SemaphoreType.DMA
    vm = pltpu.VMEM
    shapes = (
        jax.ShapeDtypeStruct((896, 384), BF16),
        jax.ShapeDtypeStruct((14, 384), F32),
        jax.ShapeDtypeStruct((14, 384), F32),
    )
    results = pl.pallas_call(
        kernel,
        out_shape=shapes,
        in_specs=[any_spec, any_spec, any_spec, vmem_spec, vmem_spec, vmem_spec],
        out_specs=(any_spec, vmem_spec, vmem_spec),
        scratch_shapes=[
            vm((1024, 896), BF16), vm((896, 384), jnp.int32), vm((128, 384), BF16),
            vm((896, 384), BF16), vm((1024, 1024), BF16), vm((896, 1024), BF16),
            vm((16, 384), F32), vm((16, 384), F32), vm((16, 384), F32), vm((16, 384), F32),
            vm((NJ, 1024, W), BF16), vm((NJ, 1024, W), BF16),
            vm((NJ, 1024, 2 * W), BF16), vm((NJ, 896, W), BF16),
            vm((7, 128, 384), BF16), vm((7, 128, 384), BF16),
            vm((NJ, 7, 128, W), BF16), vm((NJ, 7, 128, W), BF16),
            vm((2, 128, 384), F32), vm((256, 384), F32),
            vm((NJ, 2, 128, W), F32), vm((NJ, 256, W), F32),
            vm((2, 128, 384), F32), vm((NJ, 2, 128, W), F32), vm((128, 384), F32),
            vm((NJ, 512, 2 * W), BF16), vm((NJ, 512, 2 * W), BF16), vm((NJ, 8, 4, 16, 2 * W), F32),
            vm((NJ, 2, 8, 4, 16, W), BF16), vm((NJ, 7, 4, 16, W), BF16), vm((NJ, 3, 8, 16, W), BF16),
            vm((NJ, 4, 16, W), F32), vm((NJ, 8, 16, W), F32),
            vm((NJ, 4, 16, W), BF16), vm((NJ, 8, 16, W), BF16),
            vm((NJ, 3, 16, W), BF16), vm((NJ, 7, 16, W), BF16),
            dma((9,)), dma((4, 7)), dma((4, 7)), dma((NJ, 7)), dma((NJ, 7)),
            dma((2, NJ)), dma((2, NJ)), dma((2, NJ)), dma((2, NJ)),
            dma((NJ,)), dma((NJ,)), dma((NJ, 4)), dma((NJ, 4)),
        ],
        compiler_params=pltpu.CompilerParams(
            collective_id=0, has_side_effects=True, vmem_limit_bytes=56 * 2**20
        ),
        name="sophia",
    )(acts, targets, probe, master, moment, curv)
    return pl.pallas_call(
        copy_kernel,
        out_shape=shapes,
        in_specs=[vmem_spec] * 3,
        out_specs=(vmem_spec,) * 3,
        name="write_out",
    )(*results)


def solution(mesh):
    in_specs = (
        P("dp", "tensor"),
        P("dp", None),
        P("tensor", None),
        P(("tensor", "dp"), None),
        P(("tensor", "dp"), None),
        P(("tensor", "dp"), None),
    )
    out_specs = (P("tensor", None), P(("tensor", "dp"), None), P(("tensor", "dp"), None))
    return jax.shard_map(body, mesh=mesh, in_specs=in_specs, out_specs=out_specs, check_vma=False)
```

time: 110 us -> 93.3 us (0.85)
  Pallas kernels: 105 us -> 92.5 us
  local copies, waits for them, and re-layouts: 4.71 us -> 0 us
    pallas_call x1 -> x2, Pallas kernels: 105 us -> 92.5 us  [the longest x1 90.4 us: body(): pl.pallas_call(kernel, out_shape=shapes, in_specs=[any_spec, any_spec, an...]
    unnamed x3 -> x0, local copies, waits for them, and re-layouts: 4.71 us -> none
where the time goes in v2:
time: 93.3 us; the launch traced here: 93.1 us
  Pallas kernels  92.5 us (99%)
    pallas_call x1, Pallas kernels, body(): pl.pallas_call(kernel, out_shape=shapes, in_specs=[any_spec, any_spec, an...  90.4 us
    pallas_call x1, Pallas kernels, body(): pl.pallas_call(copy_kernel, out_shape=shapes, in_specs=[vmem_spec] * 3, o...  2.03 us

profile of v2, /device:TPU:1, one launch (start us, length us, event | category | flops | bytes accessed | tf_op | source)
XLA Modules:
  0.0 93.1 jit_solution(12520480542445944919)
XLA Ops:
  0.6 90.4 %sophia.1 = (bf16[896,384]{1,0:T(8,128)(2,1)}, f32[14,384]{1,0:T(8,128)}, f32[14,384]{1,0:T(8,128)}) custom-call(bf16[1024,896]{1,0:T(8,128)(2,1)} %acts_hbm.1, bf16[1024,384]{1,0:T(8,128)(2,1)} %targets_hbm.1, s32[896,384]{1,0:T(8,128)} %probe_hbm.1, f32[14,384]{1,0:T(8,128)} %master_ref.1, f32[14,384]{1,0:T(8,128)} %moment_ref.1, f32[14,384]{1,0:T(8,128)} %curv_ref.1), custom_call_target="tpu_custom_call" | custom-call | tf_op jit(solution)/shard_map/sophia/pallas_call | solution.py:410
  91.1 2.0 %write_out.1 = (bf16[896,384]{1,0:T(8,128)(2,1)}, f32[14,384]{1,0:T(8,128)}, f32[14,384]{1,0:T(8,128)}) custom-call(bf16[896,384]{1,0:T(8,128)(2,1)} %get-tuple-element.6.refs_0_, f32[14,384]{1,0:T(8,128)} %get-tuple-element.7.refs_1_, f32[14,384]{1,0:T(8,128)} %get-tuple-element.8.refs_2_), custom_call_target="tpu_custom_call" | custom-call | tf_op jit(solution)/shard_map/write_out/pallas_call | solution.py:440

commit v3 on v2

--- a/solution.py
+++ b/solution.py
@@ -12,7 +12,7 @@
 BF16 = jnp.bfloat16
 NJ = 3
 W = 128
-A_, B_, C_, D_, E_, F_, Z_ = range(7)
+A_, B_, C_, D_, E_, F_ = range(6)
 
 
 def mm(a, b):
@@ -29,9 +29,9 @@
     acts, probe, targets, signs, acts_pad, sel_t,
     master16, moment16, curv16, signs16,
     wbuf, nbuf, sig, obuf,
-    s0, r0, s1, r1, keep0, own0, keep1, own1, tot0, tot1, probed,
+    s0, r0, s1, r1, keep0, own0, keep1, own1, tot0, tot1, swap_out, swap_in,
     dsend, drecv, town, tsend, recv_a1, recv_b1, sum_a, sum_b, send_a2, send_b2, recv_a2, recv_b2,
-    local_sem, rs_ss, rs_rs, ag_ss, ag_rs,
+    local_sem, rs_ss, rs_rs, sw_ss, sw_rs, ag_ss, ag_rs,
     wa_ss, wa_rs, wc_ss, wc_rs, d_ss, d_rs, t_ss, t_rs,
 ):
     inverse = 1.0 / math.sqrt(acts_hbm.shape[0] * lax.axis_size("dp"))
@@ -97,8 +97,7 @@
         )
         load.start()
         act_loads.append(load)
-    my_rows = pl.ds(pl.multiple_of(x * 256 + zh * 128, 128), 128)
-    target_load = pltpu.make_async_copy(targets_hbm.at[my_rows, :], targets, local_sem.at[5])
+    target_load = pltpu.make_async_copy(targets_hbm.at[rows256(x), :], targets, local_sem.at[5])
     target_load.start()
 
     barrier = pltpu.get_barrier_semaphore()
@@ -196,51 +195,50 @@
         sb, rb, keep, own, tot = bufs(g)
         for kind in (C_, D_, E_, F_):
             reduce_got(g, kind)
-        tot[0] = own[0:128, :] + rb[E_].astype(F32) + rb[D_].astype(F32)
-        tot[1] = own[128:256, :] + rb[C_].astype(F32) + rb[F_].astype(F32)
-        sb[Z_] = tot[1 - zh].astype(BF16)
-        reduce_send(g, Z_, to_zh)
-
-    def reduce_4(g):
-        sb, rb, keep, own, tot = bufs(g)
-        reduce_got(g, Z_)
-        return tot[zh] + rb[Z_].astype(F32)
-
-    def piece(q, h):
-        return pl.ds(pl.multiple_of(q * 256 + h * 128, 128), 128)
+        tot[0:128, :] = own[0:128, :] + rb[E_].astype(F32) + rb[D_].astype(F32)
+        tot[128:256, :] = own[128:256, :] + rb[C_].astype(F32) + rb[F_].astype(F32)
+        if g == 0:
+            for j in range(NJ):
+                swap_out[0, j] = tot[:, j * W : (j + 1) * W].astype(BF16)
+        else:
+            swap_out[1, g - 1] = tot[...].astype(BF16)
+            swap(1, g - 1)
+
+    def swap(k, j):
+        send(swap_out.at[k, j], swap_in.at[k, j], (sw_ss, sw_rs, (k, j)), to_zh)
+
+    def swapped(k, j, own):
+        arrived(swap_in.at[k, j], sw_rs, (k, j))
+        return own + swap_in[k, j].astype(F32)
 
     def signal_send(j, q, h, idx, to):
-        rows = piece(q, h)
-        send(sig.at[j, rows], sig.at[j, rows], (ag_ss, ag_rs, (j, idx,)), to)
+        rows = pl.ds(pl.multiple_of(q * 256 + h * 128, 128), 128)
+        send(sig.at[j, rows], sig.at[j, rows], (ag_ss, ag_rs, (j, idx)), to)
 
     def signal_got(j, idx):
-        arrived(sig.at[j, pl.ds(0, 128)], ag_rs, (j, idx,))
+        arrived(sig.at[j, pl.ds(0, 128)], ag_rs, (j, idx))
 
     def signal_a(j):
-        out = reduce_4(1 + j)
         cols = slice(j * W, (j + 1) * W)
+        probed = swapped(0, j, tot0[:, cols])
+        out = swapped(1, j, tot1[j])
         slope = jnp.tanh(out - targets[:, cols].astype(F32))
-        bend = (1.0 - slope * slope) * probed[:, cols]
-        rows = piece(x, zh)
-        sig[j, rows, 0:W] = (slope * inverse).astype(BF16)
-        sig[j, rows, W : 2 * W] = (bend * inverse).astype(BF16)
-        signal_send(j, x, zh, 0, to_zh)
-        signal_send(j, x, zh, 1 + zh, to_right)
-        signal_send(j, x, zh, 3 + zh, to_left)
-
-    def signal_b(j):
+        bend = (1.0 - slope * slope) * probed
+        sig[j, rows256(x), 0:W] = (slope * inverse).astype(BF16)
+        sig[j, rows256(x), W : 2 * W] = (bend * inverse).astype(BF16)
+        signal_send(j, x, 0, 0, to_right)
+        signal_send(j, x, 1, 3, to_left)
+        signal_send(j, x, 1, 1, to_right)
+        signal_send(j, x, 0, 2, to_left)
+
+    def signal_c(j):
         signal_got(j, 0)
-        signal_send(j, x, 1 - zh, 2 - zh, to_right)
-        signal_send(j, x, 1 - zh, 4 - zh, to_left)
-
-    def signal_c(j):
-        signal_got(j, 1)
-        signal_send(j, left, 0, 5, to_right)
-        signal_got(j, 4)
-        signal_send(j, right, 1, 6, to_left)
+        signal_send(j, left, 0, 4, to_right)
+        signal_got(j, 3)
+        signal_send(j, right, 1, 5, to_left)
 
     def signal_d(j):
-        for idx in (2, 3, 5, 6):
+        for idx in (1, 2, 4, 5):
             signal_got(j, idx)
 
     def contract(rows, j):
@@ -275,7 +273,7 @@
             recv_a1.at[j],
         )
 
-    def terms_2(j):
+    def terms_2a(j):
         arrived(recv_a1.at[j], t_rs, (j, 0))
         total = town[j, y, :, :, 0:W]
         for i in range(7):
@@ -287,6 +285,8 @@
             [(send_a2.at[j, (zl + 1 + i) % 4], recv_a2.at[j, i], to_zl[i]) for i in range(3)],
             recv_a2.at[j],
         )
+
+    def terms_2b(j):
         arrived(recv_b1.at[j], t_rs, (j, 1))
         total = town[j, :, zl, :, W : 2 * W]
         for i in range(3):
@@ -360,26 +360,22 @@
         k = lax.broadcasted_iota(jnp.int32, (16, 896), 1)
         signs16[...] = mm(jnp.where(k == p, 1.0, 0.0).astype(BF16), signs[...])
 
-    def keep_probed():
-        probed[...] = reduce_4(0)
-
     steps = [
         (load_rows,), (make_signs,), (reduce_0, 0), (meet,),
         (gather_all, wbuf, 0, 0), (reduce_1, 0), (gather_all, wbuf, 0, 1),
-        (gather_all, wbuf, 0, 2),
         (make_sel_t,), (make_acts_pad, 0, 2), (reduce_2, 0), (make_acts_pad, 2, 4),
-        (make_signs16,), (gather_core, wbuf, 0, 0), (reduce_3, 0), (gathered, wbuf, 0, 0),
-        (reduce_0, 1), (reduce_1, 1), (gather_core, wbuf, 0, 1), (reduce_2, 1),
-        (gathered, wbuf, 0, 1), (reduce_0, 2), (reduce_1, 2), (gather_core, wbuf, 0, 2),
-        (keep_probed,), (reduce_3, 1), (gathered, wbuf, 0, 2), (reduce_0, 3), (reduce_1, 3),
-        (reduce_2, 2), (target_load.wait,), (reduce_2, 3), (reduce_3, 2), (signal_a, 0),
-        (reduce_3, 3), (signal_b, 0), (signal_a, 1), (signal_c, 0), (signal_a, 2),
-        (signal_b, 1), (signal_b, 2), (signal_c, 1), (signal_d, 0), (terms_core, 0),
-        (signal_c, 2), (terms_1, 0), (signal_d, 1), (terms_core, 1), (terms_1, 1),
-        (signal_d, 2), (terms_core, 2), (terms_2, 0), (terms_1, 2), (terms_2, 1), (update, 0),
-        (terms_2, 2), (update, 1), (update, 2), (gather_core, nbuf, 1, 0),
-        (gather_core, nbuf, 1, 1), (finish, 0), (finish, 1), (gather_core, nbuf, 1, 2),
-        (finish, 2),
+        (gather_all, wbuf, 0, 2), (gather_core, wbuf, 0, 0), (reduce_3, 0), (swap, 0, 0),
+        (swap, 0, 1), (gathered, wbuf, 0, 0), (reduce_0, 1), (reduce_1, 1),
+        (gather_core, wbuf, 0, 1), (reduce_2, 1), (gathered, wbuf, 0, 1), (reduce_0, 2),
+        (reduce_1, 2), (reduce_3, 1), (gather_core, wbuf, 0, 2), (gathered, wbuf, 0, 2),
+        (reduce_2, 2), (swap, 0, 2), (reduce_0, 3), (reduce_1, 3), (reduce_3, 2),
+        (reduce_2, 3), (make_signs16,), (target_load.wait,), (signal_a, 0), (reduce_3, 3),
+        (signal_c, 0), (signal_a, 1), (signal_d, 0), (terms_core, 0), (signal_c, 1),
+        (terms_1, 0), (signal_a, 2), (signal_d, 1), (terms_core, 1), (signal_c, 2),
+        (terms_1, 1), (terms_2b, 0), (terms_2a, 0), (signal_d, 2), (terms_core, 2),
+        (terms_1, 2), (terms_2a, 1), (terms_2b, 1), (update, 0), (terms_2b, 2), (terms_2a, 2),
+        (update, 1), (update, 2), (gather_core, nbuf, 1, 0), (gather_core, nbuf, 1, 1),
+        (finish, 0), (gather_core, nbuf, 1, 2), (finish, 1), (finish, 2),
     ]
     for step, *values in steps:
         step(*values)
@@ -413,22 +409,23 @@
         in_specs=[any_spec, any_spec, any_spec, vmem_spec, vmem_spec, vmem_spec],
         out_specs=(any_spec, vmem_spec, vmem_spec),
         scratch_shapes=[
-            vm((1024, 896), BF16), vm((896, 384), jnp.int32), vm((128, 384), BF16),
+            vm((1024, 896), BF16), vm((896, 384), jnp.int32), vm((256, 384), BF16),
             vm((896, 384), BF16), vm((1024, 1024), BF16), vm((896, 1024), BF16),
             vm((16, 384), F32), vm((16, 384), F32), vm((16, 384), F32), vm((16, 384), F32),
             vm((NJ, 1024, W), BF16), vm((NJ, 1024, W), BF16),
             vm((NJ, 1024, 2 * W), BF16), vm((NJ, 896, W), BF16),
-            vm((7, 128, 384), BF16), vm((7, 128, 384), BF16),
-            vm((NJ, 7, 128, W), BF16), vm((NJ, 7, 128, W), BF16),
+            vm((6, 128, 384), BF16), vm((6, 128, 384), BF16),
+            vm((NJ, 6, 128, W), BF16), vm((NJ, 6, 128, W), BF16),
             vm((2, 128, 384), F32), vm((256, 384), F32),
             vm((NJ, 2, 128, W), F32), vm((NJ, 256, W), F32),
-            vm((2, 128, 384), F32), vm((NJ, 2, 128, W), F32), vm((128, 384), F32),
+            vm((256, 384), F32), vm((NJ, 256, W), F32),
+            vm((2, NJ, 256, W), BF16), vm((2, NJ, 256, W), BF16),
             vm((NJ, 512, 2 * W), BF16), vm((NJ, 512, 2 * W), BF16), vm((NJ, 8, 4, 16, 2 * W), F32),
             vm((NJ, 2, 8, 4, 16, W), BF16), vm((NJ, 7, 4, 16, W), BF16), vm((NJ, 3, 8, 16, W), BF16),
             vm((NJ, 4, 16, W), F32), vm((NJ, 8, 16, W), F32),
             vm((NJ, 4, 16, W), BF16), vm((NJ, 8, 16, W), BF16),
             vm((NJ, 3, 16, W), BF16), vm((NJ, 7, 16, W), BF16),
-            dma((9,)), dma((4, 7)), dma((4, 7)), dma((NJ, 7)), dma((NJ, 7)),
+            dma((9,)), dma((4, 6)), dma((4, 6)), dma((2, NJ)), dma((2, NJ)), dma((NJ, 6)), dma((NJ, 6)),
             dma((2, NJ)), dma((2, NJ)), dma((2, NJ)), dma((2, NJ)),
             dma((NJ,)), dma((NJ,)), dma((NJ, 4)), dma((NJ, 4)),
         ],

time: 93.3 us -> 91.1 us (0.976)
  Pallas kernels: 92.5 us -> 90.3 us
    pallas_call x1, Pallas kernels: 90.4 us -> 88.3 us  [body(): pl.pallas_call(kernel, out_shape=shapes, in_specs=[any_spec, any_spec, an...]
where the time goes in v3:
time: 91.1 us; the launch traced here: 90.9 us
  Pallas kernels  90.3 us (99%)
    pallas_call x1, Pallas kernels, body(): pl.pallas_call(kernel, out_shape=shapes, in_specs=[any_spec, any_spec, an...  88.3 us
    pallas_call x1, Pallas kernels, body(): pl.pallas_call(copy_kernel, out_shape=shapes, in_specs=[vmem_spec] * 3, o...  2.03 us

profile of v3, /device:TPU:1, one launch (start us, length us, event | category | flops | bytes accessed | tf_op | source)
XLA Modules:
  0.0 90.9 jit_solution(5471250352077258709)
XLA Ops:
  0.6 88.3 %sophia.1 = (bf16[896,384]{1,0:T(8,128)(2,1)}, f32[14,384]{1,0:T(8,128)}, f32[14,384]{1,0:T(8,128)}) custom-call(bf16[1024,896]{1,0:T(8,128)(2,1)} %acts_hbm.1, bf16[1024,384]{1,0:T(8,128)(2,1)} %targets_hbm.1, s32[896,384]{1,0:T(8,128)} %probe_hbm.1, f32[14,384]{1,0:T(8,128)} %master_ref.1, f32[14,384]{1,0:T(8,128)} %moment_ref.1, f32[14,384]{1,0:T(8,128)} %curv_ref.1), custom_call_target="tpu_custom_call" | custom-call | tf_op jit(solution)/shard_map/sophia/pallas_call | solution.py:406
  88.9 2.0 %write_out.1 = (bf16[896,384]{1,0:T(8,128)(2,1)}, f32[14,384]{1,0:T(8,128)}, f32[14,384]{1,0:T(8,128)}) custom-call(bf16[896,384]{1,0:T(8,128)(2,1)} %get-tuple-element.6.refs_0_, f32[14,384]{1,0:T(8,128)} %get-tuple-element.7.refs_1_, f32[14,384]{1,0:T(8,128)} %get-tuple-element.8.refs_2_), custom_call_target="tpu_custom_call" | custom-call | tf_op jit(solution)/shard_map/write_out/pallas_call | solution.py:437

commit v4 on v3

--- a/solution.py
+++ b/solution.py
@@ -54,17 +54,6 @@
     to_zl = [dev(zl_=(zl + i) % 4) for i in range(1, 4)]
     to_y = [dev(y_=(y + i) % 8) for i in range(1, 8)]
 
-    def ring(i):
-        return (y + 4 + i // 4) % 8, (zl + 2 + i % 4) % 4
-
-    def each_peer(send_to):
-        def visit(i, _):
-            i = i + jnp.where(i >= 18, 1, 0)
-            send_to(i, *ring(i))
-            return 0
-
-        lax.fori_loop(0, 31, visit, 0)
-
     own16 = pl.multiple_of(c * 512 + y * 64 + zl * 16, 16)
     own512 = pl.multiple_of(c * 512, 512)
 
@@ -101,17 +90,12 @@
     target_load.start()
 
     barrier = pltpu.get_barrier_semaphore()
-    near = [to_right, to_left, to_zh, to_core]
-    for to in near:
+    partners = [to_right, to_left, to_zh, to_core] + to_zl + to_y
+    for to in partners:
         pl.semaphore_signal(barrier, inc=1, device_id=to, device_id_type=MESH)
 
-    def greet(i, y_, zl_):
-        pl.semaphore_signal(barrier, inc=1, device_id=dev(y_=y_, zl_=zl_), device_id_type=MESH)
-
-    each_peer(greet)
-
     def meet():
-        pl.semaphore_wait(barrier, len(near) + 31)
+        pl.semaphore_wait(barrier, len(partners))
 
     def load_rows():
         for padded, ref in ((master16, master_ref), (moment16, moment_ref), (curv16, curv_ref)):
@@ -119,29 +103,36 @@
             padded[0:14, :] = ref[...]
         low = master16[...].astype(BF16)
         for j in range(NJ):
-            wbuf[j, pl.ds(own16, 16), :] = low[:, j * W : (j + 1) * W]
-
-    def gather_all(buf, k, j, count=1):
-        rows = pl.ds(own16, 16)
-        js = pl.ds(j, count)
-
-        def visit(i, y_, zl_):
-            rcopy(
-                buf.at[js, rows], buf.at[js, rows], wa_ss.at[k, j], wa_rs.at[k, j],
-                dev(y_=y_, zl_=zl_),
-            ).start()
-
-        each_peer(visit)
-        bulk.append((buf.at[js, pl.ds(0, 496)], wa_ss, (k, j)))
-
-    def gather_core(buf, k, j, count=1):
-        js = pl.ds(j, count)
-        arrived(buf.at[js, pl.ds(0, 496)], wa_rs, (k, j))
-        rows = pl.ds(own512, 512)
-        send(buf.at[js, rows], buf.at[js, rows], (wc_ss, wc_rs, (k, j)), to_core)
-
-    def gathered(buf, k, j, count=1):
-        arrived(buf.at[pl.ds(j, count), pl.ds(0, 512)], wc_rs, (k, j))
+            wbuf[j, c, y, zl] = low[:, j * W : (j + 1) * W]
+
+    def spread(copies, whole, sems):
+        ss, rs, at = sems
+        for src, dst, to in copies:
+            rcopy(src, dst, ss.at[at], rs.at[at], to).start()
+        bulk.append((whole, ss, at))
+
+    def gather_1(buf, k, j):
+        own = buf.at[j, c, y, zl]
+        peers = to_y if j == 1 else to_zl
+        whole = buf.at[j, 0, 0:7, 0] if j == 1 else buf.at[j, 0, 0, 0:3]
+        spread([(own, own, to) for to in peers], whole, (wa_ss, wa_rs, (k, j, 0)))
+
+    def gather_2(buf, k, j):
+        if j == 1:
+            arrived(buf.at[j, 0, 0:7, 0], wa_rs, (k, j, 0))
+            block, peers, whole = buf.at[j, c, :, zl], to_zl, buf.at[j, 0, :, 0:3]
+        else:
+            arrived(buf.at[j, 0, 0, 0:3], wa_rs, (k, j, 0))
+            block, peers, whole = buf.at[j, c, y], to_y, buf.at[j, 0, 0:7]
+        spread([(block, block, to) for to in peers], whole, (wa_ss, wa_rs, (k, j, 1)))
+
+    def gather_core(buf, k, j):
+        whole = buf.at[j, 0, :, 0:3] if j == 1 else buf.at[j, 0, 0:7]
+        arrived(whole, wa_rs, (k, j, 1))
+        send(buf.at[j, c], buf.at[j, c], (wc_ss, wc_rs, (k, j)), to_core)
+
+    def gathered(buf, k, j):
+        arrived(buf.at[j, 0], wc_rs, (k, j))
 
     def bufs(g):
         if g == 0:
@@ -152,7 +143,7 @@
         if g == 0:
             load.wait()
             return mm(acts[rows256(q), :], signs[...])
-        return mm(acts_pad[rows256(q), :], wbuf[g - 1])
+        return mm(acts_pad[rows256(q), :], wbuf[g - 1].reshape(1024, W))
 
     def reduce_send(g, kind, to):
         sb, rb = bufs(g)[:2]
@@ -251,26 +242,19 @@
         send(dsend.at[j], drecv.at[j], (d_ss, d_rs, (j,)), to_core)
         town[j] = contract(pl.ds(own512, 512), j).reshape(8, 4, 16, 2 * W)
 
-    def bulk_send(j, phase, pairs, whole):
-        for src, dst, to in pairs:
-            rcopy(src, dst, t_ss.at[j, phase], t_rs.at[j, phase], to).start()
-        bulk.append((whole, t_ss, (j, phase)))
-
     def terms_1(j):
         arrived(drecv.at[j], d_rs, (j,))
         total = town[j] + drecv[j].astype(F32).reshape(8, 4, 16, 2 * W)
         town[j] = total
         tsend[j, 0] = total[..., :W].astype(BF16)
         tsend[j, 1] = total[..., W:].astype(BF16)
-        bulk_send(
-            j, 1,
+        spread(
             [(tsend.at[j, 1, :, (zl + 1 + i) % 4], recv_b1.at[j, i], to_zl[i]) for i in range(3)],
-            recv_b1.at[j],
-        )
-        bulk_send(
-            j, 0,
+            recv_b1.at[j], (t_ss, t_rs, (j, 1)),
+        )
+        spread(
             [(tsend.at[j, 0, (y + 1 + i) % 8], recv_a1.at[j, i], to_y[i]) for i in range(7)],
-            recv_a1.at[j],
+            recv_a1.at[j], (t_ss, t_rs, (j, 0)),
         )
 
     def terms_2a(j):
@@ -280,10 +264,9 @@
             total = total + recv_a1[j, i].astype(F32)
         sum_a[j] = total
         send_a2[j] = total.astype(BF16)
-        bulk_send(
-            j, 2,
+        spread(
             [(send_a2.at[j, (zl + 1 + i) % 4], recv_a2.at[j, i], to_zl[i]) for i in range(3)],
-            recv_a2.at[j],
+            recv_a2.at[j], (t_ss, t_rs, (j, 2)),
         )
 
     def terms_2b(j):
@@ -293,10 +276,9 @@
             total = total + recv_b1[j, i].astype(F32)
         sum_b[j] = total
         send_b2[j] = total.astype(BF16)
-        bulk_send(
-            j, 3,
+        spread(
             [(send_b2.at[j, (y + 1 + i) % 8], recv_b2.at[j, i], to_y[i]) for i in range(7)],
-            recv_b2.at[j],
+            recv_b2.at[j], (t_ss, t_rs, (j, 3)),
         )
 
     def update(j):
@@ -318,14 +300,14 @@
         master = master16[:, cols]
         updated = master - 0.02 * (step + 0.1 * master)
         real = lax.broadcasted_iota(jnp.int32, updated.shape, 0) < 14
-        nbuf[j, pl.ds(own16, 16), :] = jnp.where(real, updated, 0.0).astype(BF16)
-        gather_all(nbuf, 1, j)
+        nbuf[j, c, y, zl] = jnp.where(real, updated, 0.0).astype(BF16)
+        gather_1(nbuf, 1, j)
 
     stores = []
 
     def finish(j):
         gathered(nbuf, 1, j)
-        obuf[j] = mm(sel_t[...], nbuf[j]).astype(BF16)
+        obuf[j] = mm(sel_t[...], nbuf[j].reshape(1024, W)).astype(BF16)
         store = pltpu.make_async_copy(
             obuf.at[j], new_hbm.at[:, pl.ds(j * W, W)], local_sem.at[6 + j]
         )
@@ -362,19 +344,20 @@
 
     steps = [
         (load_rows,), (make_signs,), (reduce_0, 0), (meet,),
-        (gather_all, wbuf, 0, 0), (reduce_1, 0), (gather_all, wbuf, 0, 1),
-        (make_sel_t,), (make_acts_pad, 0, 2), (reduce_2, 0), (make_acts_pad, 2, 4),
-        (gather_all, wbuf, 0, 2), (gather_core, wbuf, 0, 0), (reduce_3, 0), (swap, 0, 0),
-        (swap, 0, 1), (gathered, wbuf, 0, 0), (reduce_0, 1), (reduce_1, 1),
-        (gather_core, wbuf, 0, 1), (reduce_2, 1), (gathered, wbuf, 0, 1), (reduce_0, 2),
-        (reduce_1, 2), (reduce_3, 1), (gather_core, wbuf, 0, 2), (gathered, wbuf, 0, 2),
-        (reduce_2, 2), (swap, 0, 2), (reduce_0, 3), (reduce_1, 3), (reduce_3, 2),
-        (reduce_2, 3), (make_signs16,), (target_load.wait,), (signal_a, 0), (reduce_3, 3),
-        (signal_c, 0), (signal_a, 1), (signal_d, 0), (terms_core, 0), (signal_c, 1),
-        (terms_1, 0), (signal_a, 2), (signal_d, 1), (terms_core, 1), (signal_c, 2),
-        (terms_1, 1), (terms_2b, 0), (terms_2a, 0), (signal_d, 2), (terms_core, 2),
-        (terms_1, 2), (terms_2a, 1), (terms_2b, 1), (update, 0), (terms_2b, 2), (terms_2a, 2),
-        (update, 1), (update, 2), (gather_core, nbuf, 1, 0), (gather_core, nbuf, 1, 1),
+        (gather_1, wbuf, 0, 0), (gather_1, wbuf, 0, 1), (gather_1, wbuf, 0, 2), (reduce_1, 0),
+        (gather_2, wbuf, 0, 0), (gather_2, wbuf, 0, 1), (reduce_2, 0), (gather_2, wbuf, 0, 2),
+        (make_sel_t,), (make_acts_pad, 0, 4), (gather_core, wbuf, 0, 0), (reduce_3, 0),
+        (gather_core, wbuf, 0, 1), (swap, 0, 0), (gathered, wbuf, 0, 0), (reduce_0, 1),
+        (reduce_1, 1), (gather_core, wbuf, 0, 2), (gathered, wbuf, 0, 1), (swap, 0, 1),
+        (reduce_0, 2), (reduce_1, 2), (reduce_2, 1), (gathered, wbuf, 0, 2), (reduce_2, 2),
+        (reduce_3, 1), (reduce_0, 3), (reduce_1, 3), (reduce_3, 2), (swap, 0, 2),
+        (reduce_2, 3), (make_signs16,), (target_load.wait,), (reduce_3, 3), (signal_a, 0),
+        (signal_a, 1), (signal_c, 0), (signal_c, 1), (signal_a, 2), (signal_d, 0),
+        (terms_core, 0), (signal_d, 1), (terms_core, 1), (signal_c, 2), (terms_1, 0),
+        (terms_1, 1), (signal_d, 2), (terms_core, 2), (terms_1, 2), (terms_2b, 0),
+        (terms_2a, 0), (terms_2b, 1), (terms_2a, 1), (terms_2b, 2), (terms_2a, 2),
+        (update, 0), (update, 1), (update, 2), (gather_2, nbuf, 1, 0), (gather_2, nbuf, 1, 1),
+        (gather_2, nbuf, 1, 2), (gather_core, nbuf, 1, 0), (gather_core, nbuf, 1, 1),
         (finish, 0), (gather_core, nbuf, 1, 2), (finish, 1), (finish, 2),
     ]
     for step, *values in steps:
@@ -412,7 +395,7 @@
             vm((1024, 896), BF16), vm((896, 384), jnp.int32), vm((256, 384), BF16),
             vm((896, 384), BF16), vm((1024, 1024), BF16), vm((896, 1024), BF16),
             vm((16, 384), F32), vm((16, 384), F32), vm((16, 384), F32), vm((16, 384), F32),
-            vm((NJ, 1024, W), BF16), vm((NJ, 1024, W), BF16),
+            vm((NJ, 2, 8, 4, 16, W), BF16), vm((NJ, 2, 8, 4, 16, W), BF16),
             vm((NJ, 1024, 2 * W), BF16), vm((NJ, 896, W), BF16),
             vm((6, 128, 384), BF16), vm((6, 128, 384), BF16),
             vm((NJ, 6, 128, W), BF16), vm((NJ, 6, 128, W), BF16),
@@ -426,7 +409,7 @@
             vm((NJ, 4, 16, W), BF16), vm((NJ, 8, 16, W), BF16),
             vm((NJ, 3, 16, W), BF16), vm((NJ, 7, 16, W), BF16),
             dma((9,)), dma((4, 6)), dma((4, 6)), dma((2, NJ)), dma((2, NJ)), dma((NJ, 6)), dma((NJ, 6)),
-            dma((2, NJ)), dma((2, NJ)), dma((2, NJ)), dma((2, NJ)),
+            dma((2, NJ, 2)), dma((2, NJ, 2)), dma((2, NJ)), dma((2, NJ)),
             dma((NJ,)), dma((NJ,)), dma((NJ, 4)), dma((NJ, 4)),
         ],
         compiler_params=pltpu.CompilerParams(

time: 91.1 us -> 89.1 us (0.978)
  Pallas kernels: 90.3 us -> 88.2 us
    pallas_call x1, Pallas kernels: 88.3 us -> 86.2 us  [body(): pl.pallas_call(kernel, out_shape=shapes, in_specs=[any_spec, any_spec, an...]
where the time goes in v4:
time: 89.1 us; the launch traced here: 88.9 us
  Pallas kernels  88.2 us (99%)
    pallas_call x1, Pallas kernels, body(): pl.pallas_call(kernel, out_shape=shapes, in_specs=[any_spec, any_spec, an...  86.2 us
    pallas_call x1, Pallas kernels, body(): pl.pallas_call(copy_kernel, out_shape=shapes, in_specs=[vmem_spec] * 3, o...  2.03 us

profile of v4, /device:TPU:1, one launch (start us, length us, event | category | flops | bytes accessed | tf_op | source)
XLA Modules:
  0.0 88.9 jit_solution(14059908947548619764)
XLA Ops:
  0.6 86.2 %sophia.1 = (bf16[896,384]{1,0:T(8,128)(2,1)}, f32[14,384]{1,0:T(8,128)}, f32[14,384]{1,0:T(8,128)}) custom-call(bf16[1024,896]{1,0:T(8,128)(2,1)} %acts_hbm.1, bf16[1024,384]{1,0:T(8,128)(2,1)} %targets_hbm.1, s32[896,384]{1,0:T(8,128)} %probe_hbm.1, f32[14,384]{1,0:T(8,128)} %master_ref.1, f32[14,384]{1,0:T(8,128)} %moment_ref.1, f32[14,384]{1,0:T(8,128)} %curv_ref.1), custom_call_target="tpu_custom_call" | custom-call | tf_op jit(solution)/shard_map/sophia/pallas_call | solution.py:389
  86.8 2.0 %write_out.1 = (bf16[896,384]{1,0:T(8,128)(2,1)}, f32[14,384]{1,0:T(8,128)}, f32[14,384]{1,0:T(8,128)}) custom-call(bf16[896,384]{1,0:T(8,128)(2,1)} %get-tuple-element.6.refs_0_, f32[14,384]{1,0:T(8,128)} %get-tuple-element.7.refs_1_, f32[14,384]{1,0:T(8,128)} %get-tuple-element.8.refs_2_), custom_call_target="tpu_custom_call" | custom-call | tf_op jit(solution)/shard_map/write_out/pallas_call | solution.py:420

commit v5 on v4

--- a/solution.py
+++ b/solution.py
@@ -24,8 +24,9 @@
 
 
 def kernel(
-    acts_hbm, targets_hbm, probe_hbm, master_ref, moment_ref, curv_ref,
-    new_hbm, moment_out, curv_out,
+    acts_hbm, targets_hbm, probe_hbm, master_hbm, moment_hbm, curv_hbm,
+    new_hbm, moment_hbm_out, curv_hbm_out,
+    master_in, moment_in, curv_in, moment_out, curv_out,
     acts, probe, targets, signs, acts_pad, sel_t,
     master16, moment16, curv16, signs16,
     wbuf, nbuf, sig, obuf,
@@ -76,7 +77,18 @@
     def rows256(q):
         return pl.ds(pl.multiple_of(q * 256, 256), 256)
 
-    loads = []
+    barrier = pltpu.get_barrier_semaphore()
+    partners = [to_right, to_left, to_zh, to_core] + to_zl + to_y
+    for to in partners:
+        pl.semaphore_signal(barrier, inc=1, device_id=to, device_id_type=MESH)
+
+    state_loads = []
+    for n, (src, dst) in enumerate(
+        ((master_hbm, master_in), (moment_hbm, moment_in), (curv_hbm, curv_in))
+    ):
+        load = pltpu.make_async_copy(src, dst, local_sem.at[9 + n])
+        load.start()
+        state_loads.append(load)
     probe_load = pltpu.make_async_copy(probe_hbm, probe, local_sem.at[0])
     probe_load.start()
     act_loads = []
@@ -89,21 +101,22 @@
     target_load = pltpu.make_async_copy(targets_hbm.at[rows256(x), :], targets, local_sem.at[5])
     target_load.start()
 
-    barrier = pltpu.get_barrier_semaphore()
-    partners = [to_right, to_left, to_zh, to_core] + to_zl + to_y
-    for to in partners:
-        pl.semaphore_signal(barrier, inc=1, device_id=to, device_id_type=MESH)
-
     def meet():
         pl.semaphore_wait(barrier, len(partners))
 
     def load_rows():
-        for padded, ref in ((master16, master_ref), (moment16, moment_ref), (curv16, curv_ref)):
-            padded[...] = jnp.zeros_like(padded)
-            padded[0:14, :] = ref[...]
+        state_loads[0].wait()
+        master16[...] = jnp.zeros_like(master16)
+        master16[0:14, :] = master_in[...]
         low = master16[...].astype(BF16)
         for j in range(NJ):
             wbuf[j, c, y, zl] = low[:, j * W : (j + 1) * W]
+
+    def load_states():
+        for n, (padded, ref) in enumerate(((moment16, moment_in), (curv16, curv_in))):
+            state_loads[1 + n].wait()
+            padded[...] = jnp.zeros_like(padded)
+            padded[0:14, :] = ref[...]
 
     def spread(copies, whole, sems):
         ss, rs, at = sems
@@ -305,6 +318,12 @@
 
     stores = []
 
+    def store_states():
+        for n, (src, dst) in enumerate(((moment_out, moment_hbm_out), (curv_out, curv_hbm_out))):
+            store = pltpu.make_async_copy(src, dst, local_sem.at[12 + n])
+            store.start()
+            stores.append(store)
+
     def finish(j):
         gathered(nbuf, 1, j)
         obuf[j] = mm(sel_t[...], nbuf[j].reshape(1024, W)).astype(BF16)
@@ -343,20 +362,20 @@
         signs16[...] = mm(jnp.where(k == p, 1.0, 0.0).astype(BF16), signs[...])
 
     steps = [
-        (load_rows,), (make_signs,), (reduce_0, 0), (meet,),
-        (gather_1, wbuf, 0, 0), (gather_1, wbuf, 0, 1), (gather_1, wbuf, 0, 2), (reduce_1, 0),
+        (load_rows,), (meet,), (gather_1, wbuf, 0, 0), (gather_1, wbuf, 0, 1),
+        (gather_1, wbuf, 0, 2), (make_signs,), (reduce_0, 0), (reduce_1, 0),
         (gather_2, wbuf, 0, 0), (gather_2, wbuf, 0, 1), (reduce_2, 0), (gather_2, wbuf, 0, 2),
         (make_sel_t,), (make_acts_pad, 0, 4), (gather_core, wbuf, 0, 0), (reduce_3, 0),
         (gather_core, wbuf, 0, 1), (swap, 0, 0), (gathered, wbuf, 0, 0), (reduce_0, 1),
         (reduce_1, 1), (gather_core, wbuf, 0, 2), (gathered, wbuf, 0, 1), (swap, 0, 1),
         (reduce_0, 2), (reduce_1, 2), (reduce_2, 1), (gathered, wbuf, 0, 2), (reduce_2, 2),
         (reduce_3, 1), (reduce_0, 3), (reduce_1, 3), (reduce_3, 2), (swap, 0, 2),
-        (reduce_2, 3), (make_signs16,), (target_load.wait,), (reduce_3, 3), (signal_a, 0),
+        (reduce_2, 3), (make_signs16,), (load_states,), (target_load.wait,), (reduce_3, 3), (signal_a, 0),
         (signal_a, 1), (signal_c, 0), (signal_c, 1), (signal_a, 2), (signal_d, 0),
         (terms_core, 0), (signal_d, 1), (terms_core, 1), (signal_c, 2), (terms_1, 0),
         (terms_1, 1), (signal_d, 2), (terms_core, 2), (terms_1, 2), (terms_2b, 0),
         (terms_2a, 0), (terms_2b, 1), (terms_2a, 1), (terms_2b, 2), (terms_2a, 2),
-        (update, 0), (update, 1), (update, 2), (gather_2, nbuf, 1, 0), (gather_2, nbuf, 1, 1),
+        (update, 0), (update, 1), (update, 2), (store_states,), (gather_2, nbuf, 1, 0), (gather_2, nbuf, 1, 1),
         (gather_2, nbuf, 1, 2), (gather_core, nbuf, 1, 0), (gather_core, nbuf, 1, 1),
         (finish, 0), (gather_core, nbuf, 1, 2), (finish, 1), (finish, 2),
     ]
@@ -389,9 +408,11 @@
     results = pl.pallas_call(
         kernel,
         out_shape=shapes,
-        in_specs=[any_spec, any_spec, any_spec, vmem_spec, vmem_spec, vmem_spec],
-        out_specs=(any_spec, vmem_spec, vmem_spec),
+        in_specs=[any_spec] * 6,
+        out_specs=(any_spec,) * 3,
         scratch_shapes=[
+            vm((14, 384), F32), vm((14, 384), F32), vm((14, 384), F32), vm((14, 384), F32),
+            vm((14, 384), F32),
             vm((1024, 896), BF16), vm((896, 384), jnp.int32), vm((256, 384), BF16),
             vm((896, 384), BF16), vm((1024, 1024), BF16), vm((896, 1024), BF16),
             vm((16, 384), F32), vm((16, 384), F32), vm((16, 384), F32), vm((16, 384), F32),
@@ -408,7 +429,7 @@
             vm((NJ, 4, 16, W), F32), vm((NJ, 8, 16, W), F32),
             vm((NJ, 4, 16, W), BF16), vm((NJ, 8, 16, W), BF16),
             vm((NJ, 3, 16, W), BF16), vm((NJ, 7, 16, W), BF16),
-            dma((9,)), dma((4, 6)), dma((4, 6)), dma((2, NJ)), dma((2, NJ)), dma((NJ, 6)), dma((NJ, 6)),
+            dma((14,)), dma((4, 6)), dma((4, 6)), dma((2, NJ)), dma((2, NJ)), dma((NJ, 6)), dma((NJ, 6)),
             dma((2, NJ, 2)), dma((2, NJ, 2)), dma((2, NJ)), dma((2, NJ)),
             dma((NJ,)), dma((NJ,)), dma((NJ, 4)), dma((NJ, 4)),
         ],

time: 89.1 us -> 87.9 us (0.987)
  Pallas kernels: 88.2 us -> 86.8 us
    pallas_call x1, Pallas kernels: 86.2 us -> 84.8 us  [body(): pl.pallas_call(kernel, out_shape=shapes, in_specs=[any_spec] * 6, out_spe...]
where the time goes in v5:
time: 87.9 us; the launch traced here: 87.5 us
  Pallas kernels  86.8 us (99%)
    pallas_call x1, Pallas kernels, body(): pl.pallas_call(kernel, out_shape=shapes, in_specs=[any_spec] * 6, out_spe...  84.8 us
    pallas_call x1, Pallas kernels, body(): pl.pallas_call(copy_kernel, out_shape=shapes, in_specs=[vmem_spec] * 3, o...  2.03 us

profile of v5, /device:TPU:1, one launch (start us, length us, event | category | flops | bytes accessed | tf_op | source)
XLA Modules:
  0.0 87.5 jit_solution(17646977082328282993)
XLA Ops:
  0.6 84.8 %sophia.1 = (bf16[896,384]{1,0:T(8,128)(2,1)}, f32[14,384]{1,0:T(8,128)}, f32[14,384]{1,0:T(8,128)}) custom-call(bf16[1024,896]{1,0:T(8,128)(2,1)} %acts_hbm.1, bf16[1024,384]{1,0:T(8,128)(2,1)} %targets_hbm.1, s32[896,384]{1,0:T(8,128)} %probe_hbm.1, f32[14,384]{1,0:T(8,128)} %master_hbm.1, f32[14,384]{1,0:T(8,128)} %moment_hbm.1, f32[14,384]{1,0:T(8,128)} %curv_hbm.1), custom_call_target="tpu_custom_call" | custom-call | tf_op jit(solution)/shard_map/sophia/pallas_call | solution.py:408
  85.4 2.0 %write_out.1 = (bf16[896,384]{1,0:T(8,128)(2,1)}, f32[14,384]{1,0:T(8,128)}, f32[14,384]{1,0:T(8,128)}) custom-call(bf16[896,384]{1,0:T(8,128)(2,1)} %get-tuple-element.6.refs_0_, f32[14,384]{1,0:T(8,128)} %get-tuple-element.7.refs_1_, f32[14,384]{1,0:T(8,128)} %get-tuple-element.8.refs_2_), custom_call_target="tpu_custom_call" | custom-call | tf_op jit(solution)/shard_map/write_out/pallas_call | solution.py:441

commit v6 on v5

--- a/solution.py
+++ b/solution.py
@@ -361,6 +361,14 @@
         k = lax.broadcasted_iota(jnp.int32, (16, 896), 1)
         signs16[...] = mm(jnp.where(k == p, 1.0, 0.0).astype(BF16), signs[...])
 
+    def all_sent():
+        for copy in sent:
+            copy.wait_send()
+        for ref, ss, at in bulk:
+            rcopy(ref, ref, ss.at[at], ss.at[at], to_core).wait_send()
+        sent.clear()
+        bulk.clear()
+
     steps = [
         (load_rows,), (meet,), (gather_1, wbuf, 0, 0), (gather_1, wbuf, 0, 1),
         (gather_1, wbuf, 0, 2), (make_signs,), (reduce_0, 0), (reduce_1, 0),
@@ -377,16 +385,13 @@
         (terms_2a, 0), (terms_2b, 1), (terms_2a, 1), (terms_2b, 2), (terms_2a, 2),
         (update, 0), (update, 1), (update, 2), (store_states,), (gather_2, nbuf, 1, 0), (gather_2, nbuf, 1, 1),
         (gather_2, nbuf, 1, 2), (gather_core, nbuf, 1, 0), (gather_core, nbuf, 1, 1),
-        (finish, 0), (gather_core, nbuf, 1, 2), (finish, 1), (finish, 2),
+        (finish, 0), (all_sent,), (gather_core, nbuf, 1, 2), (finish, 1), (finish, 2),
     ]
     for step, *values in steps:
         step(*values)
     for store in stores:
         store.wait()
-    for copy in sent:
-        copy.wait_send()
-    for ref, ss, at in bulk:
-        rcopy(ref, ref, ss.at[at], ss.at[at], to_core).wait_send()
+    all_sent()
 
 
 def copy_kernel(*refs):

time: 87.9 us -> 87.7 us (level)
  no operation moved by 1% of the time
where the time goes in v6:
time: 87.7 us; the launch traced here: 87.3 us
  Pallas kernels  86.7 us (99%)
    pallas_call x1, Pallas kernels, body(): pl.pallas_call(kernel, out_shape=shapes, in_specs=[any_spec] * 6, out_spe...  84.7 us
    pallas_call x1, Pallas kernels, body(): pl.pallas_call(copy_kernel, out_shape=shapes, in_specs=[vmem_spec] * 3, o...  2.03 us

profile of v6, /device:TPU:1, one launch (start us, length us, event | category | flops | bytes accessed | tf_op | source)
XLA Modules:
  0.0 87.3 jit_solution(135565413201254700)
XLA Ops:
  0.6 84.7 %sophia.1 = (bf16[896,384]{1,0:T(8,128)(2,1)}, f32[14,384]{1,0:T(8,128)}, f32[14,384]{1,0:T(8,128)}) custom-call(bf16[1024,896]{1,0:T(8,128)(2,1)} %acts_hbm.1, bf16[1024,384]{1,0:T(8,128)(2,1)} %targets_hbm.1, s32[896,384]{1,0:T(8,128)} %probe_hbm.1, f32[14,384]{1,0:T(8,128)} %master_hbm.1, f32[14,384]{1,0:T(8,128)} %moment_hbm.1, f32[14,384]{1,0:T(8,128)} %curv_hbm.1), custom_call_target="tpu_custom_call" | custom-call | tf_op jit(solution)/shard_map/sophia/pallas_call | solution.py:413
  85.3 2.0 %write_out.1 = (bf16[896,384]{1,0:T(8,128)(2,1)}, f32[14,384]{1,0:T(8,128)}, f32[14,384]{1,0:T(8,128)}) custom-call(bf16[896,384]{1,0:T(8,128)(2,1)} %get-tuple-element.6.refs_0_, f32[14,384]{1,0:T(8,128)} %get-tuple-element.7.refs_1_, f32[14,384]{1,0:T(8,128)} %get-tuple-element.8.refs_2_), custom_call_target="tpu_custom_call" | custom-call | tf_op jit(solution)/shard_map/write_out/pallas_call | solution.py:446
